TPU v7x, 512 devices: a whole 4x8x8 slice. The times are simulated.
512 devices in a mesh: dp: 8 (over x, y_hi), fsdp: 64 (over z, y_lo, core).
Axes of the slice: x: 4, y: 8 (y_hi: 2, y_lo: 4; y = y_hi * 4 + y_lo), z: 8, core: 2. Of those that a mesh axis runs over, the one named last changes fastest.
Arguments:
- inputs: bfloat16 [16384, 4096], P('fsdp'), may hold values from -6 to 6
- grad_out: bfloat16 [16384, 14336], P('fsdp', 'dp'), may hold values from -0.3125 to 0.3125
- basis: bfloat16 [4096, 128], P(('dp', 'fsdp')), may hold values from -0.09375 to 0.09375
- moment_one: float32 [14336, 128], P(('dp', 'fsdp')), may hold values from -4 to 4
- moment_two: float32 [14336, 128], P(('dp', 'fsdp')), may hold values from 0.001 to 0.01
Outputs:
- moment_new: float32 [14336, 128], P(('dp', 'fsdp'))
- second_new: float32 [14336, 128], P(('dp', 'fsdp'))
- update: bfloat16 [4096, 14336], P(('dp', 'fsdp'))
All inputs are finite; a program needn't handle non-finite values.
Results may differ from a plain program's by a relative error of at most 0.0085.
Values may be sent and summed in bfloat16 or wider, within the bound.
No kernel may reach another device: no remote copies, remote signals or barrier semaphores. Data moves between devices by JAX's collectives and lax.ppermute only.
A program may use at most 64 MiB of HBM per device.

v0:
```python
import jax
import jax.numpy as jnp
from jax import lax
from jax.sharding import PartitionSpec as P

beta_one = 0.9
beta_two = 0.999
corr_one = 1.0 - 0.9**20
corr_two = 1.0 - 0.999**20
adam_eps = 1e-08


def shards(inputs, grad_out, basis, moment_one, moment_two):
    whole_basis = lax.all_gather(basis, ("dp", "fsdp"), axis=0, tiled=True)
    projected = jnp.dot(inputs, whole_basis, preferred_element_type=jnp.float32).astype(
        jnp.bfloat16
    )
    term = lax.dot_general(
        grad_out, projected, (((0,), (0,)), ((), ())), preferred_element_type=jnp.float32
    )
    gradient = lax.psum_scatter(
        term.astype(jnp.bfloat16).astype(jnp.float32), "fsdp", scatter_dimension=0, tiled=True
    )
    moment_new = beta_one * moment_one + (1.0 - beta_one) * gradient
    second_new = beta_two * moment_two + (1.0 - beta_two) * gradient * gradient
    direction = (moment_new / corr_one / (jnp.sqrt(second_new / corr_two) + adam_eps)).astype(
        jnp.bfloat16
    )
    update = lax.dot_general(
        basis,
        lax.all_gather(direction, ("dp", "fsdp"), axis=0, tiled=True),
        (((1,), (1,)), ((), ())),
        preferred_element_type=jnp.float32,
    ).astype(jnp.bfloat16)
    return (moment_new, second_new, update)


def solution(mesh):
    in_specs = (
        P("fsdp", None),
        P("fsdp", "dp"),
        P(("dp", "fsdp"), None),
        P(("dp", "fsdp"), None),
        P(("dp", "fsdp"), None),
    )
    out_specs = (P(("dp", "fsdp"), None), P(("dp", "fsdp"), None), P(("dp", "fsdp"), None))
    return jax.shard_map(shards, mesh=mesh, in_specs=in_specs, out_specs=out_specs, check_vma=False)
```

profile of v0, /device:TPU:8, one launch (start us, length us, event | category | flops | bytes accessed | tf_op | source)
XLA Modules:
  0.0 2117.7 jit_solution(3132109377336950773)
XLA Ops:
  7.2 0.0 copy-start
  7.2 0.0 copy-start.1
  7.2 0.0 copy-start.2
  7.2 0.0 all-gather.4.cloned.1.call-start
  7.2 0.7 all-gather.4.cloned.1.call-update
  7.9 0.0 all-reduce.3.cloned.1.call-start
  8.0 751.4 %all-gather.4.cloned.1.call-done = bf16[4096,128]{1,0:T(8,128)(2,1)} async-done(((bf16[8,128]{1,0:T(8,128)(2,1)}), bf16[4096,128]{1,0:T(8,128)(2,1)}) %all-gather.4.cloned.1.call-update) | async-done | bytes 1048592 | tf_op jit(solution)/shard_map/all_gather | solution.py:14
  759.4 0.0 copy-done
  759.4 3.5 fusion.2
  762.9 0.0 all-reduce.3.cloned.1.call-update
  762.9 0.0 all-gather.6.cloned.1.call-start
  763.0 1.3 dynamic-slice
  764.9 522.5 %all-reduce.3.cloned.1.call-done = f32[1792,128]{0,1:T(8,128)} async-done(((f32[1792,128]{0,1:T(8,128)}), f32[1792,128]{0,1:T(8,128)}) %all-reduce.3.cloned.1.call-update) | async-done | bytes 917520
  1287.4 1.0 constant_dynamic-slice_fusion
  1288.4 0.1 copy.22
  1288.4 0.0 copy-done.1
  1288.4 0.0 copy-done.2
  1288.5 0.6 fusion.4
  1289.1 0.0 all-gather.6.cloned.1.call-update
  1289.1 0.0 copy-start.3
  1289.1 811.7 %all-gather.6.cloned.1.call-done = bf16[512,28,128]{2,1,0:T(8,128)(2,1)} async-done(((bf16[1,28,128]{2,1,0:T(8,128)(2,1)}), bf16[512,28,128]{2,1,0:T(8,128)(2,1)}) %all-gather.6.cloned.1.call-update) | async-done | bytes 3670032 | tf_op jit(solution)/shard_map/all_gather | solution.py:31
  2100.8 6.6 reshape.7
  2107.4 0.0 copy-done.3
  2107.4 3.8 fusion
Async XLA Ops:
  7.2 752.2 %copy-start = (bf16[256,4096]{1,0:T(8,128)(2,1)S(1)}, bf16[256,4096]{1,0:T(8,128)(2,1)}, u32[]{:S(2)}) copy-start(bf16[256,4096]{1,0:T(8,128)(2,1)} %param.5) | copy-start | bytes 6291460
  7.2 1281.3 %copy-start.1 = (f32[28,128]{1,0:T(8,128)S(1)}, f32[28,128]{1,0:T(8,128)}, u32[]{:S(2)}) copy-start(f32[28,128]{1,0:T(8,128)} %param.9) | copy-start | bytes 43012
  7.2 1281.3 %copy-start.2 = (f32[28,128]{1,0:T(8,128)S(1)}, f32[28,128]{1,0:T(8,128)}, u32[]{:S(2)}) copy-start(f32[28,128]{1,0:T(8,128)} %param.8) | copy-start | bytes 43012
  7.2 752.2 %all-gather.4.cloned.1.call-start = ((), (), s32[]{:S(2)}) async-start(), calls=%async_computation | async-start | bytes 1050624 | tf_op jit(solution)/shard_map/all_gather | solution.py:14
  7.9 1279.5 %all-reduce.3.cloned.1.call-start = ((), (), s32[]{:S(2)}) async-start(), calls=%async_computation.2 | async-start | bytes 1835008
  762.9 1337.9 %all-gather.6.cloned.1.call-start = ((), (), s32[]{:S(2)}) async-start(), calls=%async_computation.1 | async-start | bytes 4202496 | tf_op jit(solution)/shard_map/all_gather | solution.py:31
  1289.1 818.3 %copy-start.3 = (bf16[8,128]{1,0:T(8,128)(2,1)S(1)}, bf16[8,128]{1,0:T(8,128)(2,1)}, u32[]{:S(2)}) copy-start(bf16[8,128]{1,0:T(8,128)(2,1)} %param.7) | copy-start | bytes 6148
Sparse Core Ops, SparseCore 0:
  10.2 749.1 all-gather.3
  763.0 524.3 all-reduce.2
  1290.4 810.3 all-gather.5
where the time goes:
time: 2120 us
  waiting for transfers between devices  2090 us (99%)
    all_gather x1, waiting for transfers between devices, shards(): lax.all_gather(direction, ('dp', 'fsdp'), axis=0, tiled=True)  812 us
    all_gather x1, waiting for transfers between devices, shards(): whole_basis = lax.all_gather(basis, ('dp', 'fsdp'), axis=0, tiled=True)  751 us
    unnamed x4, waiting for transfers between devices  523 us
  transfers between devices with their start and end apart: 3, of which 3 were waited for; matrix products, arithmetic and copies ran while one was open for 0% of the time, Pallas kernels for 0%

commit v1 on v0

v1 whole, which is shorter than its diff:
```python
import jax
import jax.numpy as jnp
from jax import lax
from jax.sharding import Mesh, PartitionSpec as P

beta_one = 0.9
beta_two = 0.999
corr_one = 1.0 - 0.9**20
corr_two = 1.0 - 0.999**20
adam_eps = 1e-08

bf16 = jnp.bfloat16
f32 = jnp.float32
DP = ("x", "yh")
FS = ("z", "yl", "c")
ALL = DP + FS
COL = ("yh", "z", "yl")


def spread(array, axes, count):
    return lax.all_to_all(jnp.broadcast_to(array, (count,) + array.shape), axes, 0, 0)


def shards(inputs, grad_out, basis, moment_one, moment_two):
    own_rows = spread(basis, COL, 64)
    mate_rows = lax.ppermute(own_rows, "c", [(0, 1), (1, 0)])
    first = lax.axis_index("c") == 0
    slab = jnp.concatenate(
        [jnp.where(first, own_rows, mate_rows), jnp.where(first, mate_rows, own_rows)], axis=1
    ).reshape(1024, 128)
    part = lax.dynamic_slice(inputs, (0, lax.axis_index("x") * 1024), (256, 1024))
    partial = jnp.dot(part, slab, preferred_element_type=f32).astype(bf16)
    projected = spread(partial, ("x",), 4).astype(f32).sum(0).astype(bf16)
    term = lax.dot_general(
        grad_out, projected, (((0,), (0,)), ((), ())), preferred_element_type=f32
    ).astype(bf16)
    pieces = lax.all_to_all(term.reshape(64, 28, 128), FS, 0, 0)
    gradient = pieces.astype(f32).sum(0)
    moment_new = beta_one * moment_one + (1.0 - beta_one) * gradient
    second_new = beta_two * moment_two + (1.0 - beta_two) * gradient * gradient
    direction = (moment_new / corr_one / (jnp.sqrt(second_new / corr_two) + adam_eps)).astype(bf16)
    near = spread(direction, ("x", "c"), 8).reshape(224, 128)
    block = lax.dot_general(
        own_rows.reshape(512, 128), near, (((1,), (1,)), ((), ())), preferred_element_type=f32
    ).astype(bf16)
    got = lax.all_to_all(block.reshape(64, 8, 224), COL, 0, 0)
    update = got.reshape(64, 8, 4, 56).transpose(1, 2, 0, 3).reshape(8, 14336)
    return (moment_new, second_new, update)


def solution(mesh):
    fine = Mesh(mesh.devices.reshape(4, 2, 8, 4, 2), ALL)
    in_specs = (P(FS, None), P(FS, DP), P(ALL, None), P(ALL, None), P(ALL, None))
    out_specs = (P(ALL, None), P(ALL, None), P(ALL, None))
    return jax.shard_map(shards, mesh=fine, in_specs=in_specs, out_specs=out_specs, check_vma=False)
```

time: 2120 us -> 101 us (0.05)
  waiting for transfers between devices: 2090 us -> 1.31 us
  blocking collectives: 0 us -> 90.8 us
    all_gather x2 -> x0, waiting for transfers between devices: 1560 us -> none  [the longest x1 812 us: shards(): lax.all_gather(direction, ('dp', 'fsdp'), axis=0, tiled=True)]
    unnamed x4 -> x0, waiting for transfers between devices: 523 us -> none
    all_to_all x0 -> x5, blocking collectives: none -> 90.8 us  [the longest x3 47.4 us: spread(): lax.all_to_all(jnp.broadcast_to(array, (count,) + array.shape), axes, 0, 0)]
  transfers between devices with their start and end apart: 3 -> 1, of which waited for: 3 -> 1; matrix products, arithmetic and copies ran while one was open for 0% -> 0% of each run, Pallas kernels for 0% -> 0%
where the time goes in v1:
time: 101 us
  blocking collectives  90.8 us (90%)
  local copies, waits for them, and re-layouts  3.32 us (3%)
  matrix products  2 us (2%)
  starting transfers between devices  1.91 us (2%)
  waiting for transfers between devices  1.31 us (1%)
    all_to_all x3, blocking collectives, spread(): lax.all_to_all(jnp.broadcast_to(array, (count,) + array.shape), axes, 0, 0)  47.4 us
    all_to_all x1, blocking collectives, shards(): pieces = lax.all_to_all(term.reshape(64, 28, 128), FS, 0, 0)  22.8 us
    all_to_all x1, blocking collectives, shards(): got = lax.all_to_all(block.reshape(64, 8, 224), COL, 0, 0)  20.5 us
  transfers between devices with their start and end apart: 1, of which 1 were waited for; matrix products, arithmetic and copies ran while one was open for 0% of the time, Pallas kernels for 0%

profile of v1, /device:TPU:8, one launch (start us, length us, event | category | flops | bytes accessed | tf_op | source)
XLA Modules:
  0.0 101.0 jit_solution(8085975010567365289)
XLA Ops:
  0.6 0.0 copy-start
  0.6 0.8 broadcast_in_dim.9
  1.5 28.4 %all_to_all.25 = bf16[64,8,128]{2,1,0:T(8,128)(2,1)S(1)} all-to-all(bf16[64,8,128]{2,1,0:T(8,128)(2,1)S(1)} %broadcast_in_dim.9), channel_id=1, replica_groups=mesh['x'=4,'yh'=2,'z'=8,'yl'=4,'c'=2] {'yh','z','yl'}, dimensions={0} | all-to-all | bytes 262144 | tf_op jit(solution)/shard_map/all_to_all | solution.py:21
  29.9 1.9 %collective-permute-start = (bf16[64,8,128]{2,1,0:T(8,128)(2,1)S(1)}, bf16[64,8,128]{2,1,0:T(8,128)(2,1)S(1)}, u32[]{:S(2)}, u32[]{:S(2)}) collective-permute-start(bf16[64,8,128]{2,1,0:T(8,128)(2,1)S(1)} %all_to_all.25), channel_id=1, source_target_pairs={{0,1},{1,0},{2,3},{3,2},{4,5},{5,4},{6,7},{7,6},{8,9},{9,8},{10,11... | collective-permute-start | bytes 393224 | tf_op jit(solution)/shard_map/ppermute | solution.py:26
  31.8 1.3 %collective-permute-done = bf16[64,8,128]{2,1,0:T(8,128)(2,1)S(1)} collective-permute-done((bf16[64,8,128]{2,1,0:T(8,128)(2,1)S(1)}, bf16[64,8,128]{2,1,0:T(8,128)(2,1)S(1)}, u32[]{:S(2)}, u32[]{:S(2)}) %collective-permute-start) | collective-permute-done | bytes 131104 | tf_op jit(solution)/shard_map/ppermute | solution.py:26
  33.2 0.0 copy-done
  33.2 0.3 convolution_convert_fusion.2
  33.5 11.1 %all_to_all.26 = bf16[4,256,128]{2,1,0:T(8,128)(2,1)S(1)} all-to-all(bf16[4,256,128]{2,1,0:T(8,128)(2,1)S(1)} %broadcast_in_dim.10), channel_id=1, replica_groups=mesh['x'=4,'yh'=2,'z'=8,'yl'=4,'c'=2] {'x'}, dimensions={0} | all-to-all | bytes 524288 | tf_op jit(solution)/shard_map/all_to_all | solution.py:21
  44.7 1.5 %fusion = bf16[1792,128]{0,1:T(8,128)(2,1)S(1)} fusion(bf16[256,128]{1,0:T(8,128)(2,1)S(1)} %reduce_sum.21, bf16[256,1792]{1,0:T(8,128)(2,1)} %param.6), kind=kOutput, calls=%fused_computation.1 | convolution fusion | flops 117669888 | bytes 1441792 | tf_op jit(solution)/shard_map/dot_general | solution.py:34
  46.2 0.0 copy-start.1
  46.2 0.0 copy-start.2
  46.2 0.3 copy.15
  46.4 0.1 reshape.28
  46.5 22.8 %all_to_all.27 = bf16[64,28,128]{2,1,0:T(8,128)(2,1)S(1)} all-to-all(bf16[64,28,128]{2,1,0:T(8,128)(2,1)S(1)} %reshape.28), channel_id=1, replica_groups=mesh['x'=4,'yh'=2,'z'=8,'yl'=4,'c'=2] {'z','yl','c'}, dimensions={0} | all-to-all | bytes 917504 | tf_op jit(solution)/shard_map/all_to_all | solution.py:37
  69.4 0.1 convert_reduce_fusion
  69.5 0.0 copy-done.1
  69.5 0.0 copy-done.2
  69.5 0.6 divide_convert_fusion
  70.1 8.0 %all_to_all.28 = bf16[8,28,128]{2,1,0:T(8,128)(2,1)S(1)} all-to-all(bf16[8,28,128]{2,1,0:T(8,128)(2,1)S(1)} %broadcast_in_dim.11), channel_id=1, replica_groups=mesh['x'=4,'yh'=2,'z'=8,'yl'=4,'c'=2] {'x','c'}, dimensions={0} | all-to-all | bytes 114688 | tf_op jit(solution)/shard_map/all_to_all | solution.py:21
  78.2 0.2 fusion.1
  78.4 0.1 copy.16
  78.5 20.5 %all_to_all.29 = bf16[64,8,224]{2,1,0:T(8,128)(2,1)S(1)} all-to-all(bf16[64,8,224]{2,1,0:T(8,128)(2,1)S(1)} %bitcast.18), channel_id=1, replica_groups=mesh['x'=4,'yh'=2,'z'=8,'yl'=4,'c'=2] {'yh','z','yl'}, dimensions={0} | all-to-all | bytes 458752 | tf_op jit(solution)/shard_map/all_to_all | solution.py:46
  99.1 0.3 reshape.32
  99.4 0.2 copy.17
  99.6 1.4 %reshape.33 = bf16[8,14336]{1,0:T(8,128)(2,1)} reshape(bf16[8,4,64,56]{3,2,1,0:T(8,128)(2,1)S(1)} %copy.17) | data formatting | bytes 458752 | tf_op jit(solution)/shard_map/reshape | solution.py:47
  (6 shorter events, 0.2 us)
Async XLA Ops:
  0.6 32.6 %copy-start = (bf16[256,4096]{1,0:T(8,128)(2,1)S(1)}, bf16[256,4096]{1,0:T(8,128)(2,1)}, u32[]{:S(2)}) copy-start(bf16[256,4096]{1,0:T(8,128)(2,1)} %param.5) | copy-start | bytes 6291460
  29.9 3.2 %collective-permute-start = (bf16[64,8,128]{2,1,0:T(8,128)(2,1)S(1)}, bf16[64,8,128]{2,1,0:T(8,128)(2,1)S(1)}, u32[]{:S(2)}, u32[]{:S(2)}) collective-permute-start(bf16[64,8,128]{2,1,0:T(8,128)(2,1)S(1)} %all_to_all.25), channel_id=1, source_target_pairs={{0,1},{1,0},{2,3},{3,2},{4,5},{5,4},{6,7},{7,6},{8,9},{9,8},{10,11... | collective-permute-start | bytes 393224 | tf_op jit(solution)/shard_map/ppermute | solution.py:26
  46.2 23.3 %copy-start.1 = (f32[28,128]{1,0:T(8,128)S(1)}, f32[28,128]{1,0:T(8,128)}, u32[]{:S(2)}) copy-start(f32[28,128]{1,0:T(8,128)} %param.9) | copy-start | bytes 43012
  46.2 23.3 %copy-start.2 = (f32[28,128]{1,0:T(8,128)S(1)}, f32[28,128]{1,0:T(8,128)}, u32[]{:S(2)}) copy-start(f32[28,128]{1,0:T(8,128)} %param.8) | copy-start | bytes 43012

commit v2 on v1

--- a/solution.py
+++ b/solution.py
@@ -21,20 +21,24 @@
     return lax.all_to_all(jnp.broadcast_to(array, (count,) + array.shape), axes, 0, 0)
 
 
+def over_tokens(left, right):
+    return lax.dot_general(left, right, (((0,), (0,)), ((), ())), preferred_element_type=f32)
+
+
 def shards(inputs, grad_out, basis, moment_one, moment_two):
+    mate_out = lax.ppermute(grad_out, "c", [(0, 1), (1, 0)])
     own_rows = spread(basis, COL, 64)
-    mate_rows = lax.ppermute(own_rows, "c", [(0, 1), (1, 0)])
-    first = lax.axis_index("c") == 0
-    slab = jnp.concatenate(
-        [jnp.where(first, own_rows, mate_rows), jnp.where(first, mate_rows, own_rows)], axis=1
-    ).reshape(1024, 128)
+    slab = lax.all_gather(own_rows, "c", axis=1, tiled=True).reshape(1024, 128)
     part = lax.dynamic_slice(inputs, (0, lax.axis_index("x") * 1024), (256, 1024))
     partial = jnp.dot(part, slab, preferred_element_type=f32).astype(bf16)
     projected = spread(partial, ("x",), 4).astype(f32).sum(0).astype(bf16)
-    term = lax.dot_general(
-        grad_out, projected, (((0,), (0,)), ((), ())), preferred_element_type=f32
-    ).astype(bf16)
-    pieces = lax.all_to_all(term.reshape(64, 28, 128), FS, 0, 0)
+    both = lax.all_gather(projected, "c", axis=0)
+    mate = lax.dynamic_index_in_dim(both, 1 - lax.axis_index("c"), 0, keepdims=False)
+    term = over_tokens(grad_out, projected) + over_tokens(mate_out, mate)
+    term = lax.dynamic_slice(
+        term.astype(bf16).reshape(32, 56, 128), (0, lax.axis_index("c") * 28, 0), (32, 28, 128)
+    )
+    pieces = lax.all_to_all(term, ("z", "yl"), 0, 0)
     gradient = pieces.astype(f32).sum(0)
     moment_new = beta_one * moment_one + (1.0 - beta_one) * gradient
     second_new = beta_two * moment_two + (1.0 - beta_two) * gradient * gradient

time: 101 us -> 97.5 us (0.965)
  blocking collectives: 90.8 us -> 48.7 us
  starting transfers between devices: 1.91 us -> 22.8 us
  waiting for transfers between devices: 1.31 us -> 17 us
  local copies, waits for them, and re-layouts: 3.32 us -> 4.72 us
    all_to_all x3 -> x1, blocking collectives: 47.4 us -> 8 us  [spread(): lax.all_to_all(jnp.broadcast_to(array, (count,) + array.shape), axes, 0, 0)]
    all_to_all x0 -> x2, starting transfers between devices: none -> 20.9 us  [spread(): lax.all_to_all(jnp.broadcast_to(array, (count,) + array.shape), axes, 0, 0)]
    all_to_all x0 -> x2, waiting for transfers between devices: none -> 17 us  [spread(): lax.all_to_all(jnp.broadcast_to(array, (count,) + array.shape), axes, 0, 0)]
    all_to_all x1, blocking collectives: 22.8 us -> 16.3 us  [shards(): pieces = lax.all_to_all(term, ('z', 'yl'), 0, 0)]
    all_gather x0 -> x2, blocking collectives: none -> 3.88 us  [the longest x1 1.98 us: shards(): slab = lax.all_gather(own_rows, 'c', axis=1, tiled=True).reshape(1024, 128)]
    broadcast_in_dim x3, local copies, waits for them, and re-layouts: 0.89 us -> 2.26 us  [spread(): jnp.broadcast_to(array, (count,) + array.shape)]
    ppermute x1, waiting for transfers between devices: 1.31 us -> 0.01 us  [shards(): mate_out = lax.ppermute(grad_out, 'c', [(0, 1), (1, 0)])]
  transfers between devices with their start and end apart: 1 -> 3, of which waited for: 1 -> 2; matrix products, arithmetic and copies ran while one was open for 0% -> 1% of each run, Pallas kernels for 0% -> 0%
where the time goes in v2:
time: 97.5 us; the launch traced here: 97.1 us
  blocking collectives  48.7 us (50%)
  starting transfers between devices  22.8 us (23%)
  waiting for transfers between devices  17 us (17%)
  local copies, waits for them, and re-layouts  4.72 us (5%)
  matrix products  2.32 us (2%)
    all_to_all x2, starting transfers between devices, spread(): lax.all_to_all(jnp.broadcast_to(array, (count,) + array.shape), axes, 0, 0)  20.9 us
    all_to_all x1, blocking collectives, shards(): got = lax.all_to_all(block.reshape(64, 8, 224), COL, 0, 0)  20.5 us
    all_to_all x2, waiting for transfers between devices, spread(): lax.all_to_all(jnp.broadcast_to(array, (count,) + array.shape), axes, 0, 0)  17 us
    all_to_all x1, blocking collectives, shards(): pieces = lax.all_to_all(term, ('z', 'yl'), 0, 0)  16.3 us
    all_to_all x1, blocking collectives, spread(): lax.all_to_all(jnp.broadcast_to(array, (count,) + array.shape), axes, 0, 0)  8 us
    broadcast_in_dim x3, local copies, waits for them, and re-layouts, spread(): jnp.broadcast_to(array, (count,) + array.shape)  2.26 us
    all_gather x1, blocking collectives, shards(): slab = lax.all_gather(own_rows, 'c', axis=1, tiled=True).reshape(1024, 128)  1.98 us
  transfers between devices with their start and end apart: 3, of which 2 were waited for; matrix products, arithmetic and copies ran while one was open for 1% of the time, Pallas kernels for 0%

profile of v2, /device:TPU:8, one launch (start us, length us, event | category | flops | bytes accessed | tf_op | source)
XLA Modules:
  0.0 97.1 jit_solution(7106887976632887382)
XLA Ops:
  0.6 0.0 copy-start
  0.6 0.0 copy-start.1
  0.7 1.5 %broadcast_in_dim.9 = bf16[64,8,128]{2,1,0:T(8,128)(2,1)} broadcast(bf16[8,128]{1,0:T(8,128)(2,1)} %param.7), dimensions={1,2} | broadcast | bytes 133120 | tf_op jit(solution)/shard_map/broadcast_in_dim | solution.py:21
  2.2 16.6 %all-to-all-start = ((bf16[64,8,128]{2,1,0:T(8,128)(2,1)}), bf16[64,8,128]{2,1,0:T(8,128)(2,1)S(1)}, u32[]{:S(2)}, u32[]{:S(2)}) async-start(bf16[64,8,128]{2,1,0:T(8,128)(2,1)} %broadcast_in_dim.9), calls=%async_computation | async-start | bytes 262144 | tf_op jit(solution)/shard_map/all_to_all | solution.py:21
  18.8 1.9 %collective-permute-start = (bf16[256,1792]{1,0:T(8,128)(2,1)}, bf16[256,1792]{1,0:T(8,128)(2,1)}, u32[]{:S(2)}, u32[]{:S(2)}) collective-permute-start(bf16[256,1792]{1,0:T(8,128)(2,1)} %param.6), channel_id=1, source_target_pairs={{0,1},{1,0},{2,3},{3,2},{4,5},{5,4},{6,7},{7,6},{8,9},{9,8},{10,11... | collective-permute-start | bytes 2752520 | tf_op jit(solution)/shard_map/ppermute | solution.py:29
  20.7 10.1 %all-to-all-done = bf16[64,8,128]{2,1,0:T(8,128)(2,1)S(1)} async-done(((bf16[64,8,128]{2,1,0:T(8,128)(2,1)}), bf16[64,8,128]{2,1,0:T(8,128)(2,1)S(1)}, u32[]{:S(2)}, u32[]{:S(2)}) %all-to-all-start) | async-done | bytes 131104 | tf_op jit(solution)/shard_map/all_to_all | solution.py:21
  30.7 2.0 %all_gather.9 = bf16[64,16,128]{2,1,0:T(8,128)(2,1)S(1)} all-gather(bf16[64,8,128]{2,1,0:T(8,128)(2,1)S(1)} %all-to-all-done), channel_id=1, replica_groups=mesh['x'=4,'yh'=2,'z'=8,'yl'=4,'c'=2] {'c'}, dimensions={1}, use_global_device_ids=true | all-gather | bytes 393216 | tf_op jit(solution)/shard_map/all_gather | solution.py:31
  32.7 0.0 copy-done
  32.7 0.3 convolution_convert_fusion.1
  33.0 0.7 broadcast_in_dim.10
  33.8 4.3 %all-to-all-start.1 = ((bf16[4,256,128]{2,1,0:T(8,128)(2,1)}), bf16[4,256,128]{2,1,0:T(8,128)(2,1)S(1)}, u32[]{:S(2)}, u32[]{:S(2)}) async-start(bf16[4,256,128]{2,1,0:T(8,128)(2,1)} %broadcast_in_dim.10), calls=%async_computation.1 | async-start | bytes 524288 | tf_op jit(solution)/shard_map/all_to_all | solution.py:21
  38.1 7.0 %all-to-all-done.1 = bf16[4,256,128]{2,1,0:T(8,128)(2,1)S(1)} async-done(((bf16[4,256,128]{2,1,0:T(8,128)(2,1)}), bf16[4,256,128]{2,1,0:T(8,128)(2,1)S(1)}, u32[]{:S(2)}, u32[]{:S(2)}) %all-to-all-start.1) | async-done | bytes 262176 | tf_op jit(solution)/shard_map/all_to_all | solution.py:21
  45.1 1.9 %all-gather = bf16[512,128]{1,0:T(8,128)(2,1)S(1)} all-gather(bf16[256,128]{1,0:T(8,128)(2,1)S(1)} %reduce_sum.21), channel_id=2, replica_groups=mesh['x'=4,'yh'=2,'z'=8,'yl'=4,'c'=2] {'c'}, dimensions={0}, use_global_device_ids=true | all-gather | bytes 196608 | tf_op jit(solution)/shard_map/all_gather | solution.py:35
  47.0 0.0 copy-done.1
  47.0 0.3 fusion.11
  47.3 0.0 collective-permute-done
  47.3 0.0 copy-start.2
  47.3 0.0 copy-start.3
  47.3 1.5 %fusion.1 = bf16[1792,128]{0,1:T(8,128)(2,1)S(1)} fusion(f32[128,1792]{1,0:T(8,128)S(1)} %fusion.11, bf16[256,1792]{1,0:T(8,128)(2,1)} %collective-permute-done, bf16[2,256,128]{2,1,0:T(8,128)(2,1)S(1)} %bitcast.26, s32[]{:T(128)S(6)} %select_n.11), kind=kOutput, calls=%fused_computation.2 | convolution fusion | flops 117899264 | bytes 2359300 | tf_op jit(solution)/shard_map/dot_general | solution.py:25
  48.8 0.3 copy.15
  49.1 0.1 constant_dynamic-slice_fusion
  49.2 16.3 %all_to_all.25 = bf16[32,28,128]{2,1,0:T(8,128)(2,1)S(1)} all-to-all(bf16[32,28,128]{2,1,0:T(8,128)(2,1)S(1)} %constant_dynamic-slice_fusion), channel_id=1, replica_groups=mesh['x'=4,'yh'=2,'z'=8,'yl'=4,'c'=2] {'z','yl'}, dimensions={0} | all-to-all | bytes 458752 | tf_op jit(solution)/shard_map/all_to_all | solution.py:41
  65.5 0.1 convert_reduce_fusion
  65.6 0.0 copy-done.2
  65.6 0.0 copy-done.3
  65.6 0.6 divide_convert_fusion
  66.2 8.0 %all_to_all.26 = bf16[8,28,128]{2,1,0:T(8,128)(2,1)S(1)} all-to-all(bf16[8,28,128]{2,1,0:T(8,128)(2,1)S(1)} %broadcast_in_dim.11), channel_id=1, replica_groups=mesh['x'=4,'yh'=2,'z'=8,'yl'=4,'c'=2] {'x','c'}, dimensions={0} | all-to-all | bytes 114688 | tf_op jit(solution)/shard_map/all_to_all | solution.py:21
  74.3 0.2 fusion.2
  74.5 0.1 copy.16
  74.6 20.5 %all_to_all.27 = bf16[64,8,224]{2,1,0:T(8,128)(2,1)S(1)} all-to-all(bf16[64,8,224]{2,1,0:T(8,128)(2,1)S(1)} %bitcast.25), channel_id=1, replica_groups=mesh['x'=4,'yh'=2,'z'=8,'yl'=4,'c'=2] {'yh','z','yl'}, dimensions={0} | all-to-all | bytes 458752 | tf_op jit(solution)/shard_map/all_to_all | solution.py:50
  95.2 0.3 reshape.32
  95.4 0.2 copy.17
  95.7 1.4 %reshape.33 = bf16[8,14336]{1,0:T(8,128)(2,1)} reshape(bf16[8,4,64,56]{3,2,1,0:T(8,128)(2,1)S(1)} %copy.17) | data formatting | bytes 458752 | tf_op jit(solution)/shard_map/reshape | solution.py:51
  (3 shorter events, 0.1 us)
Async XLA Ops:
  0.6 32.1 %copy-start = (bf16[256,4096]{1,0:T(8,128)(2,1)S(1)}, bf16[256,4096]{1,0:T(8,128)(2,1)}, u32[]{:S(2)}) copy-start(bf16[256,4096]{1,0:T(8,128)(2,1)} %param.5) | copy-start | bytes 6291460
  0.6 46.3 %copy-start.1 = (bf16[256,1792]{1,0:T(8,128)(2,1)S(1)}, bf16[256,1792]{1,0:T(8,128)(2,1)}, u32[]{:S(2)}) copy-start(bf16[256,1792]{1,0:T(8,128)(2,1)} %param.6) | copy-start | bytes 2752516
  2.2 28.6 %all-to-all-start = ((bf16[64,8,128]{2,1,0:T(8,128)(2,1)}), bf16[64,8,128]{2,1,0:T(8,128)(2,1)S(1)}, u32[]{:S(2)}, u32[]{:S(2)}) async-start(bf16[64,8,128]{2,1,0:T(8,128)(2,1)} %broadcast_in_dim.9), calls=%async_computation | async-start | bytes 262144 | tf_op jit(solution)/shard_map/all_to_all | solution.py:21
  18.8 28.6 %collective-permute-start = (bf16[256,1792]{1,0:T(8,128)(2,1)}, bf16[256,1792]{1,0:T(8,128)(2,1)}, u32[]{:S(2)}, u32[]{:S(2)}) collective-permute-start(bf16[256,1792]{1,0:T(8,128)(2,1)} %param.6), channel_id=1, source_target_pairs={{0,1},{1,0},{2,3},{3,2},{4,5},{5,4},{6,7},{7,6},{8,9},{9,8},{10,11... | collective-permute-start | bytes 2752520 | tf_op jit(solution)/shard_map/ppermute | solution.py:29
  33.8 11.3 %all-to-all-start.1 = ((bf16[4,256,128]{2,1,0:T(8,128)(2,1)}), bf16[4,256,128]{2,1,0:T(8,128)(2,1)S(1)}, u32[]{:S(2)}, u32[]{:S(2)}) async-start(bf16[4,256,128]{2,1,0:T(8,128)(2,1)} %broadcast_in_dim.10), calls=%async_computation.1 | async-start | bytes 524288 | tf_op jit(solution)/shard_map/all_to_all | solution.py:21
  47.3 18.3 %copy-start.2 = (f32[28,128]{1,0:T(8,128)S(1)}, f32[28,128]{1,0:T(8,128)}, u32[]{:S(2)}) copy-start(f32[28,128]{1,0:T(8,128)} %param.9) | copy-start | bytes 43012
  47.3 18.3 %copy-start.3 = (f32[28,128]{1,0:T(8,128)S(1)}, f32[28,128]{1,0:T(8,128)}, u32[]{:S(2)}) copy-start(f32[28,128]{1,0:T(8,128)} %param.8) | copy-start | bytes 43012

commit v3 on v2

--- a/solution.py
+++ b/solution.py
@@ -31,13 +31,13 @@
     slab = lax.all_gather(own_rows, "c", axis=1, tiled=True).reshape(1024, 128)
     part = lax.dynamic_slice(inputs, (0, lax.axis_index("x") * 1024), (256, 1024))
     partial = jnp.dot(part, slab, preferred_element_type=f32).astype(bf16)
+    partial, first = lax.optimization_barrier((partial, lax.axis_index("c") == 0))
     projected = spread(partial, ("x",), 4).astype(f32).sum(0).astype(bf16)
     both = lax.all_gather(projected, "c", axis=0)
-    mate = lax.dynamic_index_in_dim(both, 1 - lax.axis_index("c"), 0, keepdims=False)
-    term = over_tokens(grad_out, projected) + over_tokens(mate_out, mate)
-    term = lax.dynamic_slice(
-        term.astype(bf16).reshape(32, 56, 128), (0, lax.axis_index("c") * 28, 0), (32, 28, 128)
-    )
+    mate = jnp.where(first, both[1], both[0])
+    term = (over_tokens(grad_out, projected) + over_tokens(mate_out, mate)).astype(bf16)
+    term = term.reshape(32, 56, 128)
+    term = jnp.where(first, term[:, :28], term[:, 28:])
     pieces = lax.all_to_all(term, ("z", "yl"), 0, 0)
     gradient = pieces.astype(f32).sum(0)
     moment_new = beta_one * moment_one + (1.0 - beta_one) * gradient

time: 97.5 us -> 96.5 us (0.990)
  blocking collectives: 48.7 us -> 59.8 us
  waiting for transfers between devices: 17 us -> 10.1 us
  starting transfers between devices: 22.8 us -> 18.5 us
    all_to_all x1 -> x2, blocking collectives: 8 us -> 19.1 us  [spread(): lax.all_to_all(jnp.broadcast_to(array, (count,) + array.shape), axes, 0, 0)]
    all_to_all x2 -> x1, waiting for transfers between devices: 17 us -> 10.1 us  [spread(): lax.all_to_all(jnp.broadcast_to(array, (count,) + array.shape), axes, 0, 0)]
    all_to_all x2 -> x1, starting transfers between devices: 20.9 us -> 16.6 us  [spread(): lax.all_to_all(jnp.broadcast_to(array, (count,) + array.shape), axes, 0, 0)]
  transfers between devices with their start and end apart: 3 -> 2, of which waited for: 2 -> 1; matrix products, arithmetic and copies ran while one was open for 1% -> 1% of each run, Pallas kernels for 0% -> 0%
where the time goes in v3:
time: 96.5 us; the launch traced here: 96.1 us
  blocking collectives  59.8 us (62%)
  starting transfers between devices  18.5 us (19%)
  waiting for transfers between devices  10.1 us (10%)
  local copies, waits for them, and re-layouts  3.89 us (4%)
  matrix products  2.32 us (2%)
    all_to_all x1, blocking collectives, shards(): got = lax.all_to_all(block.reshape(64, 8, 224), COL, 0, 0)  20.5 us
    all_to_all x2, blocking collectives, spread(): lax.all_to_all(jnp.broadcast_to(array, (count,) + array.shape), axes, 0, 0)  19.1 us
    all_to_all x1, starting transfers between devices, spread(): lax.all_to_all(jnp.broadcast_to(array, (count,) + array.shape), axes, 0, 0)  16.6 us
    all_to_all x1, blocking collectives, shards(): pieces = lax.all_to_all(term, ('z', 'yl'), 0, 0)  16.3 us
    all_to_all x1, waiting for transfers between devices, spread(): lax.all_to_all(jnp.broadcast_to(array, (count,) + array.shape), axes, 0, 0)  10.1 us
    all_gather x1, blocking collectives, shards(): slab = lax.all_gather(own_rows, 'c', axis=1, tiled=True).reshape(1024, 128)  1.98 us
  transfers between devices with their start and end apart: 2, of which 1 were waited for; matrix products, arithmetic and copies ran while one was open for 1% of the time, Pallas kernels for 0%

profile of v3, /device:TPU:8, one launch (start us, length us, event | category | flops | bytes accessed | tf_op | source)
XLA Modules:
  0.0 96.1 jit_solution(15626411816848191726)
XLA Ops:
  0.6 0.0 copy-start
  0.6 0.0 copy-start.1
  0.7 1.5 %broadcast_in_dim.9 = bf16[64,8,128]{2,1,0:T(8,128)(2,1)} broadcast(bf16[8,128]{1,0:T(8,128)(2,1)} %param.7), dimensions={1,2} | broadcast | bytes 133120 | tf_op jit(solution)/shard_map/broadcast_in_dim | solution.py:21
  2.2 16.6 %all-to-all-start = ((bf16[64,8,128]{2,1,0:T(8,128)(2,1)}), bf16[64,8,128]{2,1,0:T(8,128)(2,1)S(1)}, u32[]{:S(2)}, u32[]{:S(2)}) async-start(bf16[64,8,128]{2,1,0:T(8,128)(2,1)} %broadcast_in_dim.9), calls=%async_computation | async-start | bytes 262144 | tf_op jit(solution)/shard_map/all_to_all | solution.py:21
  18.8 1.9 %collective-permute-start = (bf16[256,1792]{1,0:T(8,128)(2,1)}, bf16[256,1792]{1,0:T(8,128)(2,1)}, u32[]{:S(2)}, u32[]{:S(2)}) collective-permute-start(bf16[256,1792]{1,0:T(8,128)(2,1)} %param.6), channel_id=1, source_target_pairs={{0,1},{1,0},{2,3},{3,2},{4,5},{5,4},{6,7},{7,6},{8,9},{9,8},{10,11... | collective-permute-start | bytes 2752520 | tf_op jit(solution)/shard_map/ppermute | solution.py:29
  20.7 10.1 %all-to-all-done = bf16[64,8,128]{2,1,0:T(8,128)(2,1)S(1)} async-done(((bf16[64,8,128]{2,1,0:T(8,128)(2,1)}), bf16[64,8,128]{2,1,0:T(8,128)(2,1)S(1)}, u32[]{:S(2)}, u32[]{:S(2)}) %all-to-all-start) | async-done | bytes 131104 | tf_op jit(solution)/shard_map/all_to_all | solution.py:21
  30.7 2.0 %all_gather.9 = bf16[64,16,128]{2,1,0:T(8,128)(2,1)S(1)} all-gather(bf16[64,8,128]{2,1,0:T(8,128)(2,1)S(1)} %all-to-all-done), channel_id=1, replica_groups=mesh['x'=4,'yh'=2,'z'=8,'yl'=4,'c'=2] {'c'}, dimensions={1}, use_global_device_ids=true | all-gather | bytes 393216 | tf_op jit(solution)/shard_map/all_gather | solution.py:31
  32.7 0.0 copy-done
  32.7 0.3 convolution_convert_fusion.1
  33.1 11.1 %all_to_all.25 = bf16[4,256,128]{2,1,0:T(8,128)(2,1)S(1)} all-to-all(bf16[4,256,128]{2,1,0:T(8,128)(2,1)S(1)} %broadcast_in_dim.10), channel_id=1, replica_groups=mesh['x'=4,'yh'=2,'z'=8,'yl'=4,'c'=2] {'x'}, dimensions={0} | all-to-all | bytes 524288 | tf_op jit(solution)/shard_map/all_to_all | solution.py:21
  44.2 1.9 %all-gather = bf16[512,128]{1,0:T(8,128)(2,1)S(1)} all-gather(bf16[256,128]{1,0:T(8,128)(2,1)S(1)} %reduce_sum.21), channel_id=2, replica_groups=mesh['x'=4,'yh'=2,'z'=8,'yl'=4,'c'=2] {'c'}, dimensions={0}, use_global_device_ids=true | all-gather | bytes 196608 | tf_op jit(solution)/shard_map/all_gather | solution.py:36
  46.1 0.0 copy-done.1
  46.1 0.3 fusion.10
  46.4 0.0 copy-start.2
  46.4 0.0 copy-start.3
  46.4 0.0 collective-permute-done
  46.4 1.5 %fusion.1 = bf16[1792,128]{0,1:T(8,128)(2,1)S(1)} fusion(f32[128,1792]{1,0:T(8,128)S(1)} %fusion.10, bf16[256,1792]{1,0:T(8,128)(2,1)} %collective-permute-done, bf16[512,128]{1,0:T(8,128)(2,1)S(1)} %all-gather, pred[]{:T(512)S(6)} %eq.3), kind=kOutput, calls=%fused_computation.2 | convolution fusion | flops 117932032 | bytes 2424833 | tf_op jit(solution)/shard_map/dot_general | solution.py:25
  47.9 0.3 copy.15
  48.2 0.1 slice_select_fusion
  48.3 16.3 %all_to_all.26 = bf16[32,28,128]{2,1,0:T(8,128)(2,1)S(1)} all-to-all(bf16[32,28,128]{2,1,0:T(8,128)(2,1)S(1)} %slice_select_fusion), channel_id=1, replica_groups=mesh['x'=4,'yh'=2,'z'=8,'yl'=4,'c'=2] {'z','yl'}, dimensions={0} | all-to-all | bytes 458752 | tf_op jit(solution)/shard_map/all_to_all | solution.py:41
  64.6 0.1 convert_reduce_fusion
  64.7 0.0 copy-done.2
  64.7 0.0 copy-done.3
  64.7 0.6 divide_convert_fusion
  65.3 8.0 %all_to_all.27 = bf16[8,28,128]{2,1,0:T(8,128)(2,1)S(1)} all-to-all(bf16[8,28,128]{2,1,0:T(8,128)(2,1)S(1)} %broadcast_in_dim.11), channel_id=1, replica_groups=mesh['x'=4,'yh'=2,'z'=8,'yl'=4,'c'=2] {'x','c'}, dimensions={0} | all-to-all | bytes 114688 | tf_op jit(solution)/shard_map/all_to_all | solution.py:21
  73.3 0.2 fusion.2
  73.5 0.1 copy.16
  73.7 20.5 %all_to_all.28 = bf16[64,8,224]{2,1,0:T(8,128)(2,1)S(1)} all-to-all(bf16[64,8,224]{2,1,0:T(8,128)(2,1)S(1)} %bitcast.21), channel_id=1, replica_groups=mesh['x'=4,'yh'=2,'z'=8,'yl'=4,'c'=2] {'yh','z','yl'}, dimensions={0} | all-to-all | bytes 458752 | tf_op jit(solution)/shard_map/all_to_all | solution.py:50
  94.2 0.3 reshape.34
  94.5 0.2 copy.17
  94.7 1.4 %reshape.35 = bf16[8,14336]{1,0:T(8,128)(2,1)} reshape(bf16[8,4,64,56]{3,2,1,0:T(8,128)(2,1)S(1)} %copy.17) | data formatting | bytes 458752 | tf_op jit(solution)/shard_map/reshape | solution.py:51
  (4 shorter events, 0.1 us)
Async XLA Ops:
  0.6 32.1 %copy-start = (bf16[256,4096]{1,0:T(8,128)(2,1)S(1)}, bf16[256,4096]{1,0:T(8,128)(2,1)}, u32[]{:S(2)}) copy-start(bf16[256,4096]{1,0:T(8,128)(2,1)} %param.5) | copy-start | bytes 6291460
  0.6 45.4 %copy-start.1 = (bf16[256,1792]{1,0:T(8,128)(2,1)S(1)}, bf16[256,1792]{1,0:T(8,128)(2,1)}, u32[]{:S(2)}) copy-start(bf16[256,1792]{1,0:T(8,128)(2,1)} %param.6) | copy-start | bytes 2752516
  2.2 28.6 %all-to-all-start = ((bf16[64,8,128]{2,1,0:T(8,128)(2,1)}), bf16[64,8,128]{2,1,0:T(8,128)(2,1)S(1)}, u32[]{:S(2)}, u32[]{:S(2)}) async-start(bf16[64,8,128]{2,1,0:T(8,128)(2,1)} %broadcast_in_dim.9), calls=%async_computation | async-start | bytes 262144 | tf_op jit(solution)/shard_map/all_to_all | solution.py:21
  18.8 27.7 %collective-permute-start = (bf16[256,1792]{1,0:T(8,128)(2,1)}, bf16[256,1792]{1,0:T(8,128)(2,1)}, u32[]{:S(2)}, u32[]{:S(2)}) collective-permute-start(bf16[256,1792]{1,0:T(8,128)(2,1)} %param.6), channel_id=1, source_target_pairs={{0,1},{1,0},{2,3},{3,2},{4,5},{5,4},{6,7},{7,6},{8,9},{9,8},{10,11... | collective-permute-start | bytes 2752520 | tf_op jit(solution)/shard_map/ppermute | solution.py:29
  46.4 18.2 %copy-start.2 = (f32[28,128]{1,0:T(8,128)S(1)}, f32[28,128]{1,0:T(8,128)}, u32[]{:S(2)}) copy-start(f32[28,128]{1,0:T(8,128)} %param.9) | copy-start | bytes 43012
  46.4 18.2 %copy-start.3 = (f32[28,128]{1,0:T(8,128)S(1)}, f32[28,128]{1,0:T(8,128)}, u32[]{:S(2)}) copy-start(f32[28,128]{1,0:T(8,128)} %param.8) | copy-start | bytes 43012

commit v4 on v3

--- a/solution.py
+++ b/solution.py
@@ -26,18 +26,19 @@
 
 
 def shards(inputs, grad_out, basis, moment_one, moment_two):
-    mate_out = lax.ppermute(grad_out, "c", [(0, 1), (1, 0)])
     own_rows = spread(basis, COL, 64)
+    cotangent = grad_out.T
+    own_rows, cotangent = lax.optimization_barrier((own_rows, cotangent))
     slab = lax.all_gather(own_rows, "c", axis=1, tiled=True).reshape(1024, 128)
     part = lax.dynamic_slice(inputs, (0, lax.axis_index("x") * 1024), (256, 1024))
     partial = jnp.dot(part, slab, preferred_element_type=f32).astype(bf16)
     partial, first = lax.optimization_barrier((partial, lax.axis_index("c") == 0))
     projected = spread(partial, ("x",), 4).astype(f32).sum(0).astype(bf16)
-    both = lax.all_gather(projected, "c", axis=0)
-    mate = jnp.where(first, both[1], both[0])
-    term = (over_tokens(grad_out, projected) + over_tokens(mate_out, mate)).astype(bf16)
-    term = term.reshape(32, 56, 128)
-    term = jnp.where(first, term[:, :28], term[:, 28:])
+    term = jnp.dot(cotangent, projected, preferred_element_type=f32).astype(bf16).reshape(32, 56, 128)
+    even, odd = term[:, :28], term[:, 28:]
+    pair = lax.all_gather(jnp.where(first, odd, even), "c", axis=0)
+    term = jnp.where(first, even, odd).astype(f32) + jnp.where(first, pair[1], pair[0]).astype(f32)
+    term = term.astype(bf16)
     pieces = lax.all_to_all(term, ("z", "yl"), 0, 0)
     gradient = pieces.astype(f32).sum(0)
     moment_new = beta_one * moment_one + (1.0 - beta_one) * gradient

time: 96.5 us -> 95.5 us (0.990)
  waiting for transfers between devices: 10.1 us -> 12 us
  starting transfers between devices: 18.5 us -> 16.6 us
  matrix products: 2.32 us -> 0.96 us
    all_to_all x1, waiting for transfers between devices: 10.1 us -> 12 us  [spread(): lax.all_to_all(jnp.broadcast_to(array, (count,) + array.shape), axes, 0, 0)]
    ppermute x1 -> x0, starting transfers between devices: 1.92 us -> none  [shards(): mate_out = lax.ppermute(grad_out, 'c', [(0, 1), (1, 0)])]
    dot_general x2 -> x1, matrix products: 1.81 us -> 0.45 us  [shards(): jnp.dot(cotangent, projected, preferred_element_type=f32).astype(bf16)]
  transfers between devices with their start and end apart: 2 -> 1, of which waited for: 1 -> 1; matrix products, arithmetic and copies ran while one was open for 1% -> 0% of each run, Pallas kernels for 0% -> 0%
where the time goes in v4:
time: 95.5 us; the launch traced here: 95.2 us
  blocking collectives  60 us (63%)
  starting transfers between devices  16.6 us (17%)
  waiting for transfers between devices  12 us (13%)
  local copies, waits for them, and re-layouts  3.82 us (4%)
  other arithmetic  1.03 us (1%)
  matrix products  0.96 us (1%)
    all_to_all x1, blocking collectives, shards(): got = lax.all_to_all(block.reshape(64, 8, 224), COL, 0, 0)  20.5 us
    all_to_all x2, blocking collectives, spread(): lax.all_to_all(jnp.broadcast_to(array, (count,) + array.shape), axes, 0, 0)  19.1 us
    all_to_all x1, starting transfers between devices, spread(): lax.all_to_all(jnp.broadcast_to(array, (count,) + array.shape), axes, 0, 0)  16.6 us
    all_to_all x1, blocking collectives, shards(): pieces = lax.all_to_all(term, ('z', 'yl'), 0, 0)  16.3 us
    all_to_all x1, waiting for transfers between devices, spread(): lax.all_to_all(jnp.broadcast_to(array, (count,) + array.shape), axes, 0, 0)  12 us
    all_gather x1, blocking collectives, shards(): pair = lax.all_gather(jnp.where(first, odd, even), 'c', axis=0)  2.13 us
    all_gather x1, blocking collectives, shards(): slab = lax.all_gather(own_rows, 'c', axis=1, tiled=True).reshape(1024, 128)  1.98 us
  transfers between devices with their start and end apart: 1, of which 1 were waited for; matrix products, arithmetic and copies ran while one was open for 0% of the time, Pallas kernels for 0%

profile of v4, /device:TPU:8, one launch (start us, length us, event | category | flops | bytes accessed | tf_op | source)
XLA Modules:
  0.0 95.2 jit_solution(5038733690303228903)
XLA Ops:
  0.6 0.0 copy-start
  0.6 0.0 copy-start.1
  0.7 1.5 %broadcast_in_dim.9 = bf16[64,8,128]{2,1,0:T(8,128)(2,1)} broadcast(bf16[8,128]{1,0:T(8,128)(2,1)} %param.7), dimensions={1,2} | broadcast | bytes 133120 | tf_op jit(solution)/shard_map/broadcast_in_dim | solution.py:21
  2.2 16.6 %all-to-all-start = ((bf16[64,8,128]{2,1,0:T(8,128)(2,1)}), bf16[64,8,128]{2,1,0:T(8,128)(2,1)S(1)}, u32[]{:S(2)}, u32[]{:S(2)}) async-start(bf16[64,8,128]{2,1,0:T(8,128)(2,1)} %broadcast_in_dim.9), calls=%async_computation | async-start | bytes 262144 | tf_op jit(solution)/shard_map/all_to_all | solution.py:21
  18.8 12.0 %all-to-all-done = bf16[64,8,128]{2,1,0:T(8,128)(2,1)S(1)} async-done(((bf16[64,8,128]{2,1,0:T(8,128)(2,1)}), bf16[64,8,128]{2,1,0:T(8,128)(2,1)S(1)}, u32[]{:S(2)}, u32[]{:S(2)}) %all-to-all-start) | async-done | bytes 131104 | tf_op jit(solution)/shard_map/all_to_all | solution.py:21
  30.7 2.0 %all_gather.9 = bf16[64,16,128]{2,1,0:T(8,128)(2,1)S(1)} all-gather(bf16[64,8,128]{2,1,0:T(8,128)(2,1)S(1)} %all-to-all-done), channel_id=1, replica_groups=mesh['x'=4,'yh'=2,'z'=8,'yl'=4,'c'=2] {'c'}, dimensions={1}, use_global_device_ids=true | all-gather | bytes 393216 | tf_op jit(solution)/shard_map/all_gather | solution.py:32
  32.7 0.0 copy-done
  32.7 0.3 convolution_convert_fusion.2
  33.1 11.1 %all_to_all.25 = bf16[4,256,128]{2,1,0:T(8,128)(2,1)S(1)} all-to-all(bf16[4,256,128]{2,1,0:T(8,128)(2,1)S(1)} %broadcast_in_dim.10), channel_id=1, replica_groups=mesh['x'=4,'yh'=2,'z'=8,'yl'=4,'c'=2] {'x'}, dimensions={0} | all-to-all | bytes 524288 | tf_op jit(solution)/shard_map/all_to_all | solution.py:21
  44.2 0.0 copy-done.1
  44.2 0.5 convolution_convert_fusion
  44.7 0.1 fusion.6
  44.8 0.0 copy-start.2
  44.8 0.0 copy-start.3
  44.8 0.1 broadcast_select_fusion
  44.9 2.1 %all-gather = bf16[64,28,128]{2,0,1:T(8,128)(2,1)S(1)} all-gather(bf16[32,28,128]{2,0,1:T(8,128)(2,1)S(1)} %broadcast_select_fusion), channel_id=2, replica_groups=mesh['x'=4,'yh'=2,'z'=8,'yl'=4,'c'=2] {'c'}, dimensions={0}, use_global_device_ids=true | all-gather | bytes 688128 | tf_op jit(solution)/shard_map/all_gather | solution.py:39
  47.1 0.2 fusion.1
  47.2 0.1 copy.24
  47.3 16.3 %all_to_all.26 = bf16[32,28,128]{2,1,0:T(8,128)(2,1)S(1)} all-to-all(bf16[32,28,128]{2,1,0:T(8,128)(2,1)S(1)} %copy.24), channel_id=1, replica_groups=mesh['x'=4,'yh'=2,'z'=8,'yl'=4,'c'=2] {'z','yl'}, dimensions={0} | all-to-all | bytes 458752 | tf_op jit(solution)/shard_map/all_to_all | solution.py:42
  63.6 0.1 convert_reduce_fusion
  63.7 0.0 copy-done.2
  63.7 0.0 copy-done.3
  63.7 0.6 divide_convert_fusion
  64.3 8.0 %all_to_all.27 = bf16[8,28,128]{2,1,0:T(8,128)(2,1)S(1)} all-to-all(bf16[8,28,128]{2,1,0:T(8,128)(2,1)S(1)} %broadcast_in_dim.11), channel_id=1, replica_groups=mesh['x'=4,'yh'=2,'z'=8,'yl'=4,'c'=2] {'x','c'}, dimensions={0} | all-to-all | bytes 114688 | tf_op jit(solution)/shard_map/all_to_all | solution.py:21
  72.4 0.2 convolution_convert_fusion.1
  72.6 0.1 copy.25
  72.7 20.5 %all_to_all.28 = bf16[64,8,224]{2,1,0:T(8,128)(2,1)S(1)} all-to-all(bf16[64,8,224]{2,1,0:T(8,128)(2,1)S(1)} %bitcast.17), channel_id=1, replica_groups=mesh['x'=4,'yh'=2,'z'=8,'yl'=4,'c'=2] {'yh','z','yl'}, dimensions={0} | all-to-all | bytes 458752 | tf_op jit(solution)/shard_map/all_to_all | solution.py:51
  93.2 0.3 reshape.36
  93.5 0.2 copy.26
  93.7 1.4 %reshape.37 = bf16[8,14336]{1,0:T(8,128)(2,1)} reshape(bf16[8,4,64,56]{3,2,1,0:T(8,128)(2,1)S(1)} %copy.26) | data formatting | bytes 458752 | tf_op jit(solution)/shard_map/reshape | solution.py:52
  (4 shorter events, 0.1 us)
Async XLA Ops:
  0.6 32.1 %copy-start = (bf16[256,4096]{1,0:T(8,128)(2,1)S(1)}, bf16[256,4096]{1,0:T(8,128)(2,1)}, u32[]{:S(2)}) copy-start(bf16[256,4096]{1,0:T(8,128)(2,1)} %param.5) | copy-start | bytes 6291460
  0.6 43.5 %copy-start.1 = (bf16[256,1792]{1,0:T(8,128)(2,1)S(1)}, bf16[256,1792]{1,0:T(8,128)(2,1)}, u32[]{:S(2)}) copy-start(bf16[256,1792]{1,0:T(8,128)(2,1)} %param.6) | copy-start | bytes 2752516
  2.2 28.6 %all-to-all-start = ((bf16[64,8,128]{2,1,0:T(8,128)(2,1)}), bf16[64,8,128]{2,1,0:T(8,128)(2,1)S(1)}, u32[]{:S(2)}, u32[]{:S(2)}) async-start(bf16[64,8,128]{2,1,0:T(8,128)(2,1)} %broadcast_in_dim.9), calls=%async_computation | async-start | bytes 262144 | tf_op jit(solution)/shard_map/all_to_all | solution.py:21
  44.8 18.9 %copy-start.2 = (f32[28,128]{1,0:T(8,128)S(1)}, f32[28,128]{1,0:T(8,128)}, u32[]{:S(2)}) copy-start(f32[28,128]{1,0:T(8,128)} %param.9) | copy-start | bytes 43012
  44.8 18.9 %copy-start.3 = (f32[28,128]{1,0:T(8,128)S(1)}, f32[28,128]{1,0:T(8,128)}, u32[]{:S(2)}) copy-start(f32[28,128]{1,0:T(8,128)} %param.8) | copy-start | bytes 43012

commit v5 on v4

--- a/solution.py
+++ b/solution.py
@@ -26,13 +26,15 @@
 
 
 def shards(inputs, grad_out, basis, moment_one, moment_two):
+    basis, at_x, first = lax.optimization_barrier(
+        (basis, lax.axis_index("x").astype(jnp.uint32) * 1024, lax.axis_index("c") == 0)
+    )
     own_rows = spread(basis, COL, 64)
     cotangent = grad_out.T
     own_rows, cotangent = lax.optimization_barrier((own_rows, cotangent))
     slab = lax.all_gather(own_rows, "c", axis=1, tiled=True).reshape(1024, 128)
-    part = lax.dynamic_slice(inputs, (0, lax.axis_index("x") * 1024), (256, 1024))
+    part = lax.dynamic_slice(inputs, (jnp.uint32(0), at_x), (256, 1024))
     partial = jnp.dot(part, slab, preferred_element_type=f32).astype(bf16)
-    partial, first = lax.optimization_barrier((partial, lax.axis_index("c") == 0))
     projected = spread(partial, ("x",), 4).astype(f32).sum(0).astype(bf16)
     term = jnp.dot(cotangent, projected, preferred_element_type=f32).astype(bf16).reshape(32, 56, 128)
     even, odd = term[:, :28], term[:, 28:]

time: 95.5 us -> 94.9 us (level)
  blocking collectives: 60 us -> 88.5 us
  starting transfers between devices: 16.6 us -> 0 us
  waiting for transfers between devices: 12 us -> 0 us
    all_to_all x2 -> x3, blocking collectives: 19.1 us -> 47.6 us  [spread(): lax.all_to_all(jnp.broadcast_to(array, (count,) + array.shape), axes, 0, 0)]
    all_to_all x1 -> x0, starting transfers between devices: 16.6 us -> none  [spread(): lax.all_to_all(jnp.broadcast_to(array, (count,) + array.shape), axes, 0, 0)]
    all_to_all x1 -> x0, waiting for transfers between devices: 12 us -> none  [spread(): lax.all_to_all(jnp.broadcast_to(array, (count,) + array.shape), axes, 0, 0)]
  transfers between devices with their start and end apart: 1 -> 0, of which waited for: 1 -> 0; matrix products, arithmetic and copies ran while one was open for 0% -> 0% of each run, Pallas kernels for 0% -> 0%
where the time goes in v5:
time: 94.9 us; the launch traced here: 94.5 us
  blocking collectives  88.5 us (93%)
  local copies, waits for them, and re-layouts  3.16 us (3%)
  matrix products  1.04 us (1%)
  other arithmetic  1.03 us (1%)
    all_to_all x3, blocking collectives, spread(): lax.all_to_all(jnp.broadcast_to(array, (count,) + array.shape), axes, 0, 0)  47.6 us
    all_to_all x1, blocking collectives, shards(): got = lax.all_to_all(block.reshape(64, 8, 224), COL, 0, 0)  20.5 us
    all_to_all x1, blocking collectives, shards(): pieces = lax.all_to_all(term, ('z', 'yl'), 0, 0)  16.3 us
    all_gather x1, blocking collectives, shards(): pair = lax.all_gather(jnp.where(first, odd, even), 'c', axis=0)  2.13 us
    all_gather x1, blocking collectives, shards(): slab = lax.all_gather(own_rows, 'c', axis=1, tiled=True).reshape(1024, 128)  1.98 us

profile of v5, /device:TPU:8, one launch (start us, length us, event | category | flops | bytes accessed | tf_op | source)
XLA Modules:
  0.0 94.5 jit_solution(14138713431602966849)
XLA Ops:
  0.6 0.0 copy-start
  0.6 0.0 copy-start.1
  0.7 0.8 broadcast_in_dim.9
  1.5 28.5 %all_to_all.25 = bf16[64,8,128]{2,1,0:T(8,128)(2,1)S(1)} all-to-all(bf16[64,8,128]{2,1,0:T(8,128)(2,1)S(1)} %broadcast_in_dim.9), channel_id=1, replica_groups=mesh['x'=4,'yh'=2,'z'=8,'yl'=4,'c'=2] {'yh','z','yl'}, dimensions={0} | all-to-all | bytes 262144 | tf_op jit(solution)/shard_map/all_to_all | solution.py:21
  30.0 2.0 %all_gather.9 = bf16[64,16,128]{2,1,0:T(8,128)(2,1)S(1)} all-gather(bf16[64,8,128]{2,1,0:T(8,128)(2,1)S(1)} %all_to_all.25), channel_id=1, replica_groups=mesh['x'=4,'yh'=2,'z'=8,'yl'=4,'c'=2] {'c'}, dimensions={1}, use_global_device_ids=true | all-gather | bytes 393216 | tf_op jit(solution)/shard_map/all_gather | solution.py:35
  32.0 0.0 copy-done
  32.0 0.4 convolution_convert_fusion.2
  32.4 11.1 %all_to_all.26 = bf16[4,256,128]{2,1,0:T(8,128)(2,1)S(1)} all-to-all(bf16[4,256,128]{2,1,0:T(8,128)(2,1)S(1)} %broadcast_in_dim.10), channel_id=1, replica_groups=mesh['x'=4,'yh'=2,'z'=8,'yl'=4,'c'=2] {'x'}, dimensions={0} | all-to-all | bytes 524288 | tf_op jit(solution)/shard_map/all_to_all | solution.py:21
  43.5 0.0 copy-done.1
  43.5 0.5 convolution_convert_fusion
  44.0 0.1 fusion.6
  44.1 0.0 copy-start.2
  44.1 0.0 copy-start.3
  44.1 0.1 broadcast_select_fusion
  44.3 2.1 %all-gather = bf16[64,28,128]{2,0,1:T(8,128)(2,1)S(1)} all-gather(bf16[32,28,128]{2,0,1:T(8,128)(2,1)S(1)} %broadcast_select_fusion), channel_id=2, replica_groups=mesh['x'=4,'yh'=2,'z'=8,'yl'=4,'c'=2] {'c'}, dimensions={0}, use_global_device_ids=true | all-gather | bytes 688128 | tf_op jit(solution)/shard_map/all_gather | solution.py:41
  46.4 0.2 fusion.1
  46.6 0.1 copy.24
  46.7 16.3 %all_to_all.27 = bf16[32,28,128]{2,1,0:T(8,128)(2,1)S(1)} all-to-all(bf16[32,28,128]{2,1,0:T(8,128)(2,1)S(1)} %copy.24), channel_id=1, replica_groups=mesh['x'=4,'yh'=2,'z'=8,'yl'=4,'c'=2] {'z','yl'}, dimensions={0} | all-to-all | bytes 458752 | tf_op jit(solution)/shard_map/all_to_all | solution.py:44
  63.0 0.1 convert_reduce_fusion
  63.1 0.0 copy-done.2
  63.1 0.0 copy-done.3
  63.1 0.6 divide_convert_fusion
  63.7 8.0 %all_to_all.28 = bf16[8,28,128]{2,1,0:T(8,128)(2,1)S(1)} all-to-all(bf16[8,28,128]{2,1,0:T(8,128)(2,1)S(1)} %broadcast_in_dim.11), channel_id=1, replica_groups=mesh['x'=4,'yh'=2,'z'=8,'yl'=4,'c'=2] {'x','c'}, dimensions={0} | all-to-all | bytes 114688 | tf_op jit(solution)/shard_map/all_to_all | solution.py:21
  71.7 0.2 convolution_convert_fusion.1
  71.9 0.1 copy.25
  72.1 20.5 %all_to_all.29 = bf16[64,8,224]{2,1,0:T(8,128)(2,1)S(1)} all-to-all(bf16[64,8,224]{2,1,0:T(8,128)(2,1)S(1)} %bitcast.17), channel_id=1, replica_groups=mesh['x'=4,'yh'=2,'z'=8,'yl'=4,'c'=2] {'yh','z','yl'}, dimensions={0} | all-to-all | bytes 458752 | tf_op jit(solution)/shard_map/all_to_all | solution.py:53
  92.6 0.3 reshape.36
  92.9 0.2 copy.26
  93.1 1.4 %reshape.37 = bf16[8,14336]{1,0:T(8,128)(2,1)} reshape(bf16[8,4,64,56]{3,2,1,0:T(8,128)(2,1)S(1)} %copy.26) | data formatting | bytes 458752 | tf_op jit(solution)/shard_map/reshape | solution.py:54
  (4 shorter events, 0.1 us)
Async XLA Ops:
  0.6 31.4 %copy-start = (bf16[256,4096]{1,0:T(8,128)(2,1)S(1)}, bf16[256,4096]{1,0:T(8,128)(2,1)}, u32[]{:S(2)}) copy-start(bf16[256,4096]{1,0:T(8,128)(2,1)} %param.5) | copy-start | bytes 6291460
  0.6 42.9 %copy-start.1 = (bf16[256,1792]{1,0:T(8,128)(2,1)S(1)}, bf16[256,1792]{1,0:T(8,128)(2,1)}, u32[]{:S(2)}) copy-start(bf16[256,1792]{1,0:T(8,128)(2,1)} %param.6) | copy-start | bytes 2752516
  44.1 19.0 %copy-start.2 = (f32[28,128]{1,0:T(8,128)S(1)}, f32[28,128]{1,0:T(8,128)}, u32[]{:S(2)}) copy-start(f32[28,128]{1,0:T(8,128)} %param.9) | copy-start | bytes 43012
  44.1 18.9 %copy-start.3 = (f32[28,128]{1,0:T(8,128)S(1)}, f32[28,128]{1,0:T(8,128)}, u32[]{:S(2)}) copy-start(f32[28,128]{1,0:T(8,128)} %param.8) | copy-start | bytes 43012

commit v6 on v5

--- a/solution.py
+++ b/solution.py
@@ -14,7 +14,7 @@
 DP = ("x", "yh")
 FS = ("z", "yl", "c")
 ALL = DP + FS
-COL = ("yh", "z", "yl")
+COL = ("z", "yh", "yl")
 
 
 def spread(array, axes, count):
@@ -32,7 +32,8 @@
     own_rows = spread(basis, COL, 64)
     cotangent = grad_out.T
     own_rows, cotangent = lax.optimization_barrier((own_rows, cotangent))
-    slab = lax.all_gather(own_rows, "c", axis=1, tiled=True).reshape(1024, 128)
+    slab = lax.all_gather(own_rows, "c", axis=1, tiled=True)
+    slab = slab.reshape(8, 2, 64, 128).transpose(1, 0, 2, 3).reshape(1024, 128)
     part = lax.dynamic_slice(inputs, (jnp.uint32(0), at_x), (256, 1024))
     partial = jnp.dot(part, slab, preferred_element_type=f32).astype(bf16)
     projected = spread(partial, ("x",), 4).astype(f32).sum(0).astype(bf16)
@@ -50,8 +51,8 @@
     block = lax.dot_general(
         own_rows.reshape(512, 128), near, (((1,), (1,)), ((), ())), preferred_element_type=f32
     ).astype(bf16)
-    got = lax.all_to_all(block.reshape(64, 8, 224), COL, 0, 0)
-    update = got.reshape(64, 8, 4, 56).transpose(1, 2, 0, 3).reshape(8, 14336)
+    got = lax.all_to_all(block.reshape(64, 8, 224), ("z", "yh", "yl"), 0, 0)
+    update = got.reshape(8, 2, 4, 8, 4, 56).transpose(3, 4, 1, 0, 2, 5).reshape(8, 14336)
     return (moment_new, second_new, update)
 
 

time: 94.9 us -> 94.6 us (level)
  no operation moved by 1% of the time
where the time goes in v6:
time: 94.6 us; the launch traced here: 94.2 us
  blocking collectives  88.1 us (93%)
  local copies, waits for them, and re-layouts  3.25 us (3%)
  matrix products  1.04 us (1%)
  other arithmetic  1.03 us (1%)
    all_to_all x3, blocking collectives, spread(): lax.all_to_all(jnp.broadcast_to(array, (count,) + array.shape), axes, 0, 0)  47.5 us
    all_to_all x1, blocking collectives, shards(): got = lax.all_to_all(block.reshape(64, 8, 224), ('z', 'yh', 'yl'), 0, 0)  20.3 us
    all_to_all x1, blocking collectives, shards(): pieces = lax.all_to_all(term, ('z', 'yl'), 0, 0)  16.2 us
    all_gather x1, blocking collectives, shards(): pair = lax.all_gather(jnp.where(first, odd, even), 'c', axis=0)  2.13 us
    all_gather x1, blocking collectives, shards(): slab = lax.all_gather(own_rows, 'c', axis=1, tiled=True)  1.98 us

profile of v6, /device:TPU:8, one launch (start us, length us, event | category | flops | bytes accessed | tf_op | source)
XLA Modules:
  0.0 94.2 jit_solution(3564733912095635402)
XLA Ops:
  0.6 0.0 copy-start
  0.6 0.0 copy-start.1
  0.7 0.8 broadcast_in_dim.9
  1.5 28.4 %all_to_all.25 = bf16[64,8,128]{2,1,0:T(8,128)(2,1)S(1)} all-to-all(bf16[64,8,128]{2,1,0:T(8,128)(2,1)S(1)} %broadcast_in_dim.9), channel_id=1, replica_groups=mesh['x'=4,'yh'=2,'z'=8,'yl'=4,'c'=2] {'z','yh','yl'}, dimensions={0} | all-to-all | bytes 262144 | tf_op jit(solution)/shard_map/all_to_all | solution.py:21
  29.9 2.0 %all_gather.9 = bf16[64,16,128]{2,1,0:T(8,128)(2,1)S(1)} all-gather(bf16[64,8,128]{2,1,0:T(8,128)(2,1)S(1)} %all_to_all.25), channel_id=1, replica_groups=mesh['x'=4,'yh'=2,'z'=8,'yl'=4,'c'=2] {'c'}, dimensions={1}, use_global_device_ids=true | all-gather | bytes 393216 | tf_op jit(solution)/shard_map/all_gather | solution.py:35
  31.9 0.0 copy-done
  31.9 0.4 convolution_convert_fusion.2
  32.3 11.1 %all_to_all.26 = bf16[4,256,128]{2,1,0:T(8,128)(2,1)S(1)} all-to-all(bf16[4,256,128]{2,1,0:T(8,128)(2,1)S(1)} %broadcast_in_dim.10), channel_id=1, replica_groups=mesh['x'=4,'yh'=2,'z'=8,'yl'=4,'c'=2] {'x'}, dimensions={0} | all-to-all | bytes 524288 | tf_op jit(solution)/shard_map/all_to_all | solution.py:21
  43.5 0.0 copy-done.1
  43.5 0.5 convolution_convert_fusion
  43.9 0.1 fusion.6
  44.0 0.0 copy-start.2
  44.0 0.0 copy-start.3
  44.1 0.1 broadcast_select_fusion
  44.2 2.1 %all-gather = bf16[64,28,128]{2,0,1:T(8,128)(2,1)S(1)} all-gather(bf16[32,28,128]{2,0,1:T(8,128)(2,1)S(1)} %broadcast_select_fusion), channel_id=2, replica_groups=mesh['x'=4,'yh'=2,'z'=8,'yl'=4,'c'=2] {'c'}, dimensions={0}, use_global_device_ids=true | all-gather | bytes 688128 | tf_op jit(solution)/shard_map/all_gather | solution.py:42
  46.3 0.2 fusion.1
  46.5 0.1 copy.28
  46.6 16.2 %all_to_all.27 = bf16[32,28,128]{2,1,0:T(8,128)(2,1)S(1)} all-to-all(bf16[32,28,128]{2,1,0:T(8,128)(2,1)S(1)} %copy.28), channel_id=1, replica_groups=mesh['x'=4,'yh'=2,'z'=8,'yl'=4,'c'=2] {'z','yl'}, dimensions={0} | all-to-all | bytes 458752 | tf_op jit(solution)/shard_map/all_to_all | solution.py:45
  62.9 0.1 convert_reduce_fusion
  62.9 0.0 copy-done.2
  62.9 0.0 copy-done.3
  62.9 0.6 divide_convert_fusion
  63.6 8.0 %all_to_all.28 = bf16[8,28,128]{2,1,0:T(8,128)(2,1)S(1)} all-to-all(bf16[8,28,128]{2,1,0:T(8,128)(2,1)S(1)} %broadcast_in_dim.11), channel_id=1, replica_groups=mesh['x'=4,'yh'=2,'z'=8,'yl'=4,'c'=2] {'x','c'}, dimensions={0} | all-to-all | bytes 114688 | tf_op jit(solution)/shard_map/all_to_all | solution.py:21
  71.6 0.2 convolution_convert_fusion.1
  71.8 0.1 copy.29
  71.9 20.3 %all_to_all.29 = bf16[64,8,224]{2,1,0:T(8,128)(2,1)S(1)} all-to-all(bf16[64,8,224]{2,1,0:T(8,128)(2,1)S(1)} %bitcast.19), channel_id=1, replica_groups=mesh['x'=4,'yh'=2,'z'=8,'yl'=4,'c'=2] {'z','yh','yl'}, dimensions={0} | all-to-all | bytes 458752 | tf_op jit(solution)/shard_map/all_to_all | solution.py:54
  92.2 0.3 reshape.40
  92.5 0.3 copy.30
  92.8 1.4 %reshape.41 = bf16[8,14336]{1,0:T(8,128)(2,1)} reshape(bf16[8,4,2,8,4,56]{5,4,3,2,1,0:T(4,128)(2,1)S(1)} %copy.30) | data formatting | bytes 458752 | tf_op jit(solution)/shard_map/reshape | solution.py:55
  (5 shorter events, 0.1 us)
Async XLA Ops:
  0.6 31.3 %copy-start = (bf16[256,4096]{1,0:T(8,128)(2,1)S(1)}, bf16[256,4096]{1,0:T(8,128)(2,1)}, u32[]{:S(2)}) copy-start(bf16[256,4096]{1,0:T(8,128)(2,1)} %param.5) | copy-start | bytes 6291460
  0.6 42.8 %copy-start.1 = (bf16[256,1792]{1,0:T(8,128)(2,1)S(1)}, bf16[256,1792]{1,0:T(8,128)(2,1)}, u32[]{:S(2)}) copy-start(bf16[256,1792]{1,0:T(8,128)(2,1)} %param.6) | copy-start | bytes 2752516
  44.0 18.9 %copy-start.2 = (f32[28,128]{1,0:T(8,128)S(1)}, f32[28,128]{1,0:T(8,128)}, u32[]{:S(2)}) copy-start(f32[28,128]{1,0:T(8,128)} %param.9) | copy-start | bytes 43012
  44.0 18.9 %copy-start.3 = (f32[28,128]{1,0:T(8,128)S(1)}, f32[28,128]{1,0:T(8,128)}, u32[]{:S(2)}) copy-start(f32[28,128]{1,0:T(8,128)} %param.8) | copy-start | bytes 43012

commit v7 on v6

--- a/solution.py
+++ b/solution.py
@@ -1,6 +1,8 @@
 import jax
 import jax.numpy as jnp
 from jax import lax
+from jax.experimental import pallas as pl
+from jax.experimental.pallas import tpu as pltpu
 from jax.sharding import Mesh, PartitionSpec as P
 
 beta_one = 0.9
@@ -25,6 +27,35 @@
     return lax.dot_general(left, right, (((0,), (0,)), ((), ())), preferred_element_type=f32)
 
 
+def place(s):
+    return s // 4 % 8 * 8 + s // 32 * 4 + s % 4
+
+
+def lay_out(arrived, out_ref, got_ref, done):
+    copy = pltpu.make_async_copy(arrived, got_ref, done)
+    copy.start()
+    copy.wait()
+    lane = lax.broadcasted_iota(jnp.int32, (8, 128), 1)
+    for tile in range(2):
+        for group in range(4):
+            parts = [got_ref[place(group * 16 + m), :, tile * 128 : tile * 128 + 128].astype(f32) for m in range(16)]
+            for half in range(2):
+                turned = [
+                    pltpu.roll(parts[m], (m * 56 - half * 64) % 128, 1)
+                    if (m * 56 - half * 64) % 128
+                    else parts[m]
+                    for m in range(16)
+                ]
+                base = (tile * 2 + half) * 3584 + group * 896
+                for k in range(7):
+                    low = k * 128
+                    inside = [m for m in range(16) if m * 56 < low + 128 and m * 56 + 56 > low]
+                    value = turned[inside[0]]
+                    for m in inside[1:]:
+                        value = jnp.where(lane >= m * 56 - low, turned[m], value)
+                    out_ref[:, base + low : base + low + 128] = value.astype(bf16)
+
+
 def shards(inputs, grad_out, basis, moment_one, moment_two):
     basis, at_x, first = lax.optimization_barrier(
         (basis, lax.axis_index("x").astype(jnp.uint32) * 1024, lax.axis_index("c") == 0)
@@ -47,12 +78,20 @@
     moment_new = beta_one * moment_one + (1.0 - beta_one) * gradient
     second_new = beta_two * moment_two + (1.0 - beta_two) * gradient * gradient
     direction = (moment_new / corr_one / (jnp.sqrt(second_new / corr_two) + adam_eps)).astype(bf16)
-    near = spread(direction, ("x", "c"), 8).reshape(224, 128)
+    near = spread(direction, ("x", "c"), 8).reshape(4, 56, 128)
+    near = jnp.pad(near, ((0, 0), (0, 8), (0, 0))).reshape(256, 128)
     block = lax.dot_general(
         own_rows.reshape(512, 128), near, (((1,), (1,)), ((), ())), preferred_element_type=f32
     ).astype(bf16)
-    got = lax.all_to_all(block.reshape(64, 8, 224), ("z", "yh", "yl"), 0, 0)
-    update = got.reshape(8, 2, 4, 8, 4, 56).transpose(3, 4, 1, 0, 2, 5).reshape(8, 14336)
+    got = lax.all_to_all(block.reshape(64, 8, 256), COL, 0, 0)
+    update = pl.pallas_call(
+        lay_out,
+        out_shape=jax.ShapeDtypeStruct((8, 14336), bf16),
+        in_specs=[pl.BlockSpec(memory_space=pl.ANY)],
+        scratch_shapes=[pltpu.VMEM((64, 8, 256), bf16), pltpu.SemaphoreType.DMA],
+        compiler_params=pltpu.CompilerParams(vmem_limit_bytes=4 * 1024 * 1024),
+        cost_estimate=pl.CostEstimate(flops=0, bytes_accessed=500000, transcendentals=0),
+    )(got)
     return (moment_new, second_new, update)
 
 

time: 94.6 us -> 93.4 us (0.987)
  local copies, waits for them, and re-layouts: 3.25 us -> 1.15 us
    reshape x3 -> x1, local copies, waits for them, and re-layouts: 1.72 us -> 0.02 us  [shards(): near = spread(direction, ('x', 'c'), 8).reshape(4, 56, 128)]
where the time goes in v7:
time: 93.4 us; the launch traced here: 93 us
  blocking collectives  88.1 us (94%)
  local copies, waits for them, and re-layouts  1.15 us (1%)
  matrix products  1.04 us (1%)
  other arithmetic  1.03 us (1%)
    all_to_all x3, blocking collectives, spread(): lax.all_to_all(jnp.broadcast_to(array, (count,) + array.shape), axes, 0, 0)  47.5 us
    all_to_all x1, blocking collectives, shards(): got = lax.all_to_all(block.reshape(64, 8, 256), COL, 0, 0)  20.3 us
    all_to_all x1, blocking collectives, shards(): pieces = lax.all_to_all(term, ('z', 'yl'), 0, 0)  16.2 us
    all_gather x1, blocking collectives, shards(): pair = lax.all_gather(jnp.where(first, odd, even), 'c', axis=0)  2.13 us
    all_gather x1, blocking collectives, shards(): slab = lax.all_gather(own_rows, 'c', axis=1, tiled=True)  1.98 us

profile of v7, /device:TPU:8, one launch (start us, length us, event | category | flops | bytes accessed | tf_op | source)
XLA Modules:
  0.0 93.0 jit_solution(17427910703087978687)
XLA Ops:
  0.6 0.0 copy-start
  0.6 0.0 copy-start.1
  0.7 0.8 broadcast_in_dim.9
  1.5 28.4 %all_to_all.25 = bf16[64,8,128]{2,1,0:T(8,128)(2,1)S(1)} all-to-all(bf16[64,8,128]{2,1,0:T(8,128)(2,1)S(1)} %broadcast_in_dim.9), channel_id=1, replica_groups=mesh['x'=4,'yh'=2,'z'=8,'yl'=4,'c'=2] {'z','yh','yl'}, dimensions={0} | all-to-all | bytes 262144 | tf_op jit(solution)/shard_map/all_to_all | solution.py:23
  29.9 2.0 %all_gather.9 = bf16[64,16,128]{2,1,0:T(8,128)(2,1)S(1)} all-gather(bf16[64,8,128]{2,1,0:T(8,128)(2,1)S(1)} %all_to_all.25), channel_id=1, replica_groups=mesh['x'=4,'yh'=2,'z'=8,'yl'=4,'c'=2] {'c'}, dimensions={1}, use_global_device_ids=true | all-gather | bytes 393216 | tf_op jit(solution)/shard_map/all_gather | solution.py:66
  31.9 0.0 copy-done
  31.9 0.4 convolution_convert_fusion.2
  32.3 11.1 %all_to_all.26 = bf16[4,256,128]{2,1,0:T(8,128)(2,1)S(1)} all-to-all(bf16[4,256,128]{2,1,0:T(8,128)(2,1)S(1)} %broadcast_in_dim.10), channel_id=1, replica_groups=mesh['x'=4,'yh'=2,'z'=8,'yl'=4,'c'=2] {'x'}, dimensions={0} | all-to-all | bytes 524288 | tf_op jit(solution)/shard_map/all_to_all | solution.py:23
  43.5 0.0 copy-done.1
  43.5 0.5 convolution_convert_fusion
  43.9 0.1 fusion.7
  44.0 0.0 copy-start.2
  44.0 0.0 copy-start.3
  44.1 0.1 broadcast_select_fusion
  44.2 2.1 %all-gather = bf16[64,28,128]{2,0,1:T(8,128)(2,1)S(1)} all-gather(bf16[32,28,128]{2,0,1:T(8,128)(2,1)S(1)} %broadcast_select_fusion), channel_id=2, replica_groups=mesh['x'=4,'yh'=2,'z'=8,'yl'=4,'c'=2] {'c'}, dimensions={0}, use_global_device_ids=true | all-gather | bytes 688128 | tf_op jit(solution)/shard_map/all_gather | solution.py:73
  46.3 0.2 fusion.2
  46.5 0.1 copy.19
  46.6 16.2 %all_to_all.27 = bf16[32,28,128]{2,1,0:T(8,128)(2,1)S(1)} all-to-all(bf16[32,28,128]{2,1,0:T(8,128)(2,1)S(1)} %copy.19), channel_id=1, replica_groups=mesh['x'=4,'yh'=2,'z'=8,'yl'=4,'c'=2] {'z','yl'}, dimensions={0} | all-to-all | bytes 458752 | tf_op jit(solution)/shard_map/all_to_all | solution.py:76
  62.9 0.1 convert_reduce_fusion
  62.9 0.0 copy-done.2
  62.9 0.0 copy-done.3
  62.9 0.6 divide_convert_fusion
  63.6 8.0 %all_to_all.28 = bf16[8,28,128]{2,1,0:T(8,128)(2,1)S(1)} all-to-all(bf16[8,28,128]{2,1,0:T(8,128)(2,1)S(1)} %broadcast_in_dim.11), channel_id=1, replica_groups=mesh['x'=4,'yh'=2,'z'=8,'yl'=4,'c'=2] {'x','c'}, dimensions={0} | all-to-all | bytes 114688 | tf_op jit(solution)/shard_map/all_to_all | solution.py:23
  71.6 0.2 fusion
  71.8 20.3 %all_to_all.29.arrived = bf16[64,8,256]{2,1,0:T(8,128)(2,1)S(1)} all-to-all(bf16[64,8,256]{2,1,0:T(8,128)(2,1)S(1)} %fusion), channel_id=1, replica_groups=mesh['x'=4,'yh'=2,'z'=8,'yl'=4,'c'=2] {'z','yh','yl'}, dimensions={0} | all-to-all | bytes 524288 | tf_op jit(solution)/shard_map/all_to_all | solution.py:86
  92.1 0.9 shard_map.76
  (6 shorter events, 0.1 us)
Async XLA Ops:
  0.6 31.3 %copy-start = (bf16[256,4096]{1,0:T(8,128)(2,1)S(1)}, bf16[256,4096]{1,0:T(8,128)(2,1)}, u32[]{:S(2)}) copy-start(bf16[256,4096]{1,0:T(8,128)(2,1)} %param.5) | copy-start | bytes 6291460
  0.6 42.8 %copy-start.1 = (bf16[256,1792]{1,0:T(8,128)(2,1)S(1)}, bf16[256,1792]{1,0:T(8,128)(2,1)}, u32[]{:S(2)}) copy-start(bf16[256,1792]{1,0:T(8,128)(2,1)} %param.6) | copy-start | bytes 2752516
  44.0 18.9 %copy-start.2 = (f32[28,128]{1,0:T(8,128)S(1)}, f32[28,128]{1,0:T(8,128)}, u32[]{:S(2)}) copy-start(f32[28,128]{1,0:T(8,128)} %param.9) | copy-start | bytes 43012
  44.0 18.9 %copy-start.3 = (f32[28,128]{1,0:T(8,128)S(1)}, f32[28,128]{1,0:T(8,128)}, u32[]{:S(2)}) copy-start(f32[28,128]{1,0:T(8,128)} %param.8) | copy-start | bytes 43012

commit v8 on v7

--- a/solution.py
+++ b/solution.py
@@ -32,12 +32,16 @@
 
 
 def lay_out(arrived, out_ref, got_ref, done):
-    copy = pltpu.make_async_copy(arrived, got_ref, done)
-    copy.start()
-    copy.wait()
+    copies = []
+    for half in range(2):
+        rows = pl.ds(half * 32, 32)
+        copies.append(pltpu.make_async_copy(arrived.at[rows], got_ref.at[rows], done.at[half]))
+        copies[half].start()
     lane = lax.broadcasted_iota(jnp.int32, (8, 128), 1)
-    for tile in range(2):
-        for group in range(4):
+    for group in (0, 2, 1, 3):
+        if group < 2:
+            copies[group].wait()
+        for tile in range(2):
             parts = [got_ref[place(group * 16 + m), :, tile * 128 : tile * 128 + 128].astype(f32) for m in range(16)]
             for half in range(2):
                 turned = [
@@ -88,7 +92,7 @@
         lay_out,
         out_shape=jax.ShapeDtypeStruct((8, 14336), bf16),
         in_specs=[pl.BlockSpec(memory_space=pl.ANY)],
-        scratch_shapes=[pltpu.VMEM((64, 8, 256), bf16), pltpu.SemaphoreType.DMA],
+        scratch_shapes=[pltpu.VMEM((64, 8, 256), bf16), pltpu.SemaphoreType.DMA((2,))],
         compiler_params=pltpu.CompilerParams(vmem_limit_bytes=4 * 1024 * 1024),
         cost_estimate=pl.CostEstimate(flops=0, bytes_accessed=500000, transcendentals=0),
     )(got)

time: 93.4 us -> 93.7 us (level)
  no operation moved by 1% of the time
where the time goes in v8:
time: 93.7 us; the launch traced here: 93.4 us
  blocking collectives  88.1 us (94%)
  Pallas kernels  1.29 us (1%)
  local copies, waits for them, and re-layouts  1.15 us (1%)
  matrix products  1.04 us (1%)
  other arithmetic  1.03 us (1%)
    all_to_all x3, blocking collectives, spread(): lax.all_to_all(jnp.broadcast_to(array, (count,) + array.shape), axes, 0, 0)  47.5 us
    all_to_all x1, blocking collectives, shards(): got = lax.all_to_all(block.reshape(64, 8, 256), COL, 0, 0)  20.3 us
    all_to_all x1, blocking collectives, shards(): pieces = lax.all_to_all(term, ('z', 'yl'), 0, 0)  16.2 us
    all_gather x1, blocking collectives, shards(): pair = lax.all_gather(jnp.where(first, odd, even), 'c', axis=0)  2.13 us
    all_gather x1, blocking collectives, shards(): slab = lax.all_gather(own_rows, 'c', axis=1, tiled=True)  1.98 us

profile of v8, /device:TPU:8, one launch (start us, length us, event | category | flops | bytes accessed | tf_op | source)
XLA Modules:
  0.0 93.4 jit_solution(1017774721325402638)
XLA Ops:
  0.6 0.0 copy-start
  0.6 0.0 copy-start.1
  0.7 0.8 broadcast_in_dim.9
  1.5 28.4 %all_to_all.25 = bf16[64,8,128]{2,1,0:T(8,128)(2,1)S(1)} all-to-all(bf16[64,8,128]{2,1,0:T(8,128)(2,1)S(1)} %broadcast_in_dim.9), channel_id=1, replica_groups=mesh['x'=4,'yh'=2,'z'=8,'yl'=4,'c'=2] {'z','yh','yl'}, dimensions={0} | all-to-all | bytes 262144 | tf_op jit(solution)/shard_map/all_to_all | solution.py:23
  29.9 2.0 %all_gather.9 = bf16[64,16,128]{2,1,0:T(8,128)(2,1)S(1)} all-gather(bf16[64,8,128]{2,1,0:T(8,128)(2,1)S(1)} %all_to_all.25), channel_id=1, replica_groups=mesh['x'=4,'yh'=2,'z'=8,'yl'=4,'c'=2] {'c'}, dimensions={1}, use_global_device_ids=true | all-gather | bytes 393216 | tf_op jit(solution)/shard_map/all_gather | solution.py:70
  31.9 0.0 copy-done
  31.9 0.4 convolution_convert_fusion.2
  32.3 11.1 %all_to_all.26 = bf16[4,256,128]{2,1,0:T(8,128)(2,1)S(1)} all-to-all(bf16[4,256,128]{2,1,0:T(8,128)(2,1)S(1)} %broadcast_in_dim.10), channel_id=1, replica_groups=mesh['x'=4,'yh'=2,'z'=8,'yl'=4,'c'=2] {'x'}, dimensions={0} | all-to-all | bytes 524288 | tf_op jit(solution)/shard_map/all_to_all | solution.py:23
  43.5 0.0 copy-done.1
  43.5 0.5 convolution_convert_fusion
  43.9 0.1 fusion.7
  44.0 0.0 copy-start.2
  44.0 0.0 copy-start.3
  44.1 0.1 broadcast_select_fusion
  44.2 2.1 %all-gather = bf16[64,28,128]{2,0,1:T(8,128)(2,1)S(1)} all-gather(bf16[32,28,128]{2,0,1:T(8,128)(2,1)S(1)} %broadcast_select_fusion), channel_id=2, replica_groups=mesh['x'=4,'yh'=2,'z'=8,'yl'=4,'c'=2] {'c'}, dimensions={0}, use_global_device_ids=true | all-gather | bytes 688128 | tf_op jit(solution)/shard_map/all_gather | solution.py:77
  46.3 0.2 fusion.2
  46.5 0.1 copy.19
  46.6 16.2 %all_to_all.27 = bf16[32,28,128]{2,1,0:T(8,128)(2,1)S(1)} all-to-all(bf16[32,28,128]{2,1,0:T(8,128)(2,1)S(1)} %copy.19), channel_id=1, replica_groups=mesh['x'=4,'yh'=2,'z'=8,'yl'=4,'c'=2] {'z','yl'}, dimensions={0} | all-to-all | bytes 458752 | tf_op jit(solution)/shard_map/all_to_all | solution.py:80
  62.9 0.1 convert_reduce_fusion
  62.9 0.0 copy-done.2
  62.9 0.0 copy-done.3
  62.9 0.6 divide_convert_fusion
  63.6 8.0 %all_to_all.28 = bf16[8,28,128]{2,1,0:T(8,128)(2,1)S(1)} all-to-all(bf16[8,28,128]{2,1,0:T(8,128)(2,1)S(1)} %broadcast_in_dim.11), channel_id=1, replica_groups=mesh['x'=4,'yh'=2,'z'=8,'yl'=4,'c'=2] {'x','c'}, dimensions={0} | all-to-all | bytes 114688 | tf_op jit(solution)/shard_map/all_to_all | solution.py:23
  71.6 0.2 fusion
  71.8 20.3 %all_to_all.29.arrived = bf16[64,8,256]{2,1,0:T(8,128)(2,1)S(1)} all-to-all(bf16[64,8,256]{2,1,0:T(8,128)(2,1)S(1)} %fusion), channel_id=1, replica_groups=mesh['x'=4,'yh'=2,'z'=8,'yl'=4,'c'=2] {'z','yh','yl'}, dimensions={0} | all-to-all | bytes 524288 | tf_op jit(solution)/shard_map/all_to_all | solution.py:90
  92.1 1.3 %shard_map.76 = bf16[8,14336]{1,0:T(8,128)(2,1)} custom-call(bf16[64,8,256]{2,1,0:T(8,128)(2,1)S(1)} %all_to_all.29.arrived), custom_call_target="tpu_custom_call" | custom-call | bytes 500000 | tf_op jit(solution)/shard_map/pallas_call | solution.py:91
  (6 shorter events, 0.1 us)
Async XLA Ops:
  0.6 31.3 %copy-start = (bf16[256,4096]{1,0:T(8,128)(2,1)S(1)}, bf16[256,4096]{1,0:T(8,128)(2,1)}, u32[]{:S(2)}) copy-start(bf16[256,4096]{1,0:T(8,128)(2,1)} %param.5) | copy-start | bytes 6291460
  0.6 42.8 %copy-start.1 = (bf16[256,1792]{1,0:T(8,128)(2,1)S(1)}, bf16[256,1792]{1,0:T(8,128)(2,1)}, u32[]{:S(2)}) copy-start(bf16[256,1792]{1,0:T(8,128)(2,1)} %param.6) | copy-start | bytes 2752516
  44.0 18.9 %copy-start.2 = (f32[28,128]{1,0:T(8,128)S(1)}, f32[28,128]{1,0:T(8,128)}, u32[]{:S(2)}) copy-start(f32[28,128]{1,0:T(8,128)} %param.9) | copy-start | bytes 43012
  44.0 18.9 %copy-start.3 = (f32[28,128]{1,0:T(8,128)S(1)}, f32[28,128]{1,0:T(8,128)}, u32[]{:S(2)}) copy-start(f32[28,128]{1,0:T(8,128)} %param.8) | copy-start | bytes 43012
